TPU v7x, 32 devices: a whole 2x2x4 slice. The times are simulated.
32 devices in a mesh: group: 4 (over y, x), local: 8 (over z, core).
Axes of the slice: x: 2, y: 2, z: 4, core: 2. Of those that a mesh axis runs over, the one named last changes fastest.
Arguments:
- tokens: bfloat16 [4096, 3584], P(('group', 'local')), may hold values from -6 to 6
- grad_out: bfloat16 [4096, 3584], P(('group', 'local')), may hold values from -6 to 6
- expert_ids: int32 [4096, 4], P(('group', 'local')), may hold values from 0 to 31, as said below
- combine: bfloat16 [4096, 4], P(('group', 'local')), may hold values from 0.099609375 to 1
- gate_weight: bfloat16 [32, 3584, 1024], P(('group', 'local')), may hold values from -0.09375 to 0.09375
- up_weight: bfloat16 [32, 3584, 1024], P(('group', 'local')), may hold values from -0.09375 to 0.09375
- down_weight: bfloat16 [32, 1024, 3584], P(('group', 'local')), may hold values from -0.1875 to 0.1875
Outputs:
- grad_tokens: bfloat16 [4096, 3584], P(('group', 'local'))
- grad_combine: bfloat16 [4096, 4], P(('group', 'local'))
Inputs may be any that keep to these rules, and one draw needn't show every extreme that they name: `expert_ids`: each token names 4 different experts; expert e lies in node group e // 8. The first 2 experts of a token lie in one group and the other 2 in another, so a token uses 2 groups. The tokens of each device choose every group exactly 128//2 times. The tokens of one device name one expert at most 24 times, and in every draw some expert is named 24 times by the tokens of every device.
All inputs are finite; a program needn't handle non-finite values.
Results may differ from a plain program's by a relative error of at most 0.0058.
Values may be sent and summed in bfloat16 or wider, within the bound.
A program may use at most 128 MiB of HBM per device.

v0:
```python
import jax
import jax.numpy as jnp
from jax import lax
from jax.sharding import PartitionSpec as P


def expert_rows(rows_x, rows_dy, rows_p, gate_mat, up_mat, down_mat):
    gate_pre = jnp.dot(rows_x, gate_mat, preferred_element_type=jnp.float32)
    up_pre = jnp.dot(rows_x, up_mat, preferred_element_type=jnp.float32)
    sigmoid_gate = jax.nn.sigmoid(gate_pre)
    active = gate_pre * sigmoid_gate
    hidden = (active * up_pre).astype(jnp.bfloat16)
    output = jnp.dot(hidden, down_mat, preferred_element_type=jnp.float32)
    grad_weight = jnp.sum(rows_dy.astype(jnp.float32) * output, axis=1).astype(jnp.bfloat16)
    back_hidden = lax.dot_general(
        rows_dy, down_mat, (((1,), (1,)), ((), ())), preferred_element_type=jnp.float32
    )
    back_hidden = back_hidden * rows_p.astype(jnp.float32)[:, None]
    grad_gate = (
        back_hidden * up_pre * sigmoid_gate * (1.0 + gate_pre * (1.0 - sigmoid_gate))
    ).astype(jnp.bfloat16)
    grad_up = (back_hidden * active).astype(jnp.bfloat16)
    contrib = lax.dot_general(
        grad_gate, gate_mat, (((1,), (1,)), ((), ())), preferred_element_type=jnp.float32
    )
    contrib = contrib + lax.dot_general(
        grad_up, up_mat, (((1,), (1,)), ((), ())), preferred_element_type=jnp.float32
    )
    return (contrib.astype(jnp.bfloat16), grad_weight)


def local(tokens, grad_out, expert_ids, combine, gate_weight, up_weight, down_weight):
    token_rows, model_width = tokens.shape
    top_count = expert_ids.shape[1]
    group_count = lax.axis_size("group")
    local_count = lax.axis_size("local")
    expert_count = group_count * local_count
    mean_pair = token_rows * top_count // expert_count
    pair_cap = mean_pair + (mean_pair + 1) // 2
    gate_mat = gate_weight[0]
    up_mat = up_weight[0]
    down_mat = down_weight[0]
    zero_value = jnp.zeros((), jnp.bfloat16)
    assign_count = token_rows * top_count
    targets = expert_ids.reshape(assign_count)
    one_hot = (targets[:, None] == jnp.arange(expert_count, dtype=jnp.int32)[None, :]).astype(
        jnp.int32
    )
    rank_in = jnp.sum((jnp.cumsum(one_hot, axis=0) - 1) * one_hot, axis=1)
    slot_of = targets * pair_cap + rank_in
    slot_total = expert_count * pair_cap
    owner = (
        jnp.full((slot_total,), assign_count, jnp.int32)
        .at[slot_of]
        .set(jnp.arange(assign_count, dtype=jnp.int32))
    )
    filled = owner < assign_count
    safe_owner = jnp.minimum(owner, assign_count - 1)
    token_of = safe_owner // top_count
    send_x = jnp.where(filled[:, None], tokens[token_of], zero_value).reshape(
        expert_count, pair_cap, model_width
    )
    send_dy = jnp.where(filled[:, None], grad_out[token_of], zero_value).reshape(
        expert_count, pair_cap, model_width
    )
    send_p = jnp.where(filled, combine.reshape(assign_count)[safe_owner], zero_value).reshape(
        expert_count, pair_cap
    )
    rows_x = lax.all_to_all(send_x, ("group", "local"), split_axis=0, concat_axis=0, tiled=True)
    rows_dy = lax.all_to_all(send_dy, ("group", "local"), split_axis=0, concat_axis=0, tiled=True)
    rows_p = lax.all_to_all(send_p, ("group", "local"), split_axis=0, concat_axis=0, tiled=True)
    leading = rows_x.shape[:2]
    contrib, grad_weight = expert_rows(
        rows_x.reshape(-1, model_width),
        rows_dy.reshape(-1, model_width),
        rows_p.reshape(-1),
        gate_mat,
        up_mat,
        down_mat,
    )
    contrib, grad_weight = (contrib.reshape(leading + (model_width,)), grad_weight.reshape(leading))
    back_rows = lax.all_to_all(contrib, ("group", "local"), split_axis=0, concat_axis=0, tiled=True)
    back_weight = lax.all_to_all(
        grad_weight, ("group", "local"), split_axis=0, concat_axis=0, tiled=True
    )
    back_rows = back_rows.reshape(slot_total, model_width)
    terms = back_rows[slot_of].reshape(token_rows, top_count, model_width)
    grad_tokens = jnp.sum(terms.astype(jnp.float32), axis=1).astype(jnp.bfloat16)
    grad_combine = back_weight.reshape(slot_total)[slot_of].reshape(token_rows, top_count)
    return (grad_tokens, grad_combine)


def solution(mesh):
    placed = (
        P(("group", "local"), None),
        P(("group", "local"), None),
        P(("group", "local"), None),
        P(("group", "local"), None),
        P(("group", "local"), None, None),
        P(("group", "local"), None, None),
        P(("group", "local"), None, None),
    )
    return jax.shard_map(
        local,
        mesh=mesh,
        in_specs=placed,
        out_specs=(P(("group", "local"), None), P(("group", "local"), None)),
        check_vma=False,
    )
```

profile of v0, /device:TPU:0, one launch (start us, length us, event | category | flops | bytes accessed | tf_op | source)
XLA Modules:
  0.0 506.1 jit_solution(16559293093348464959)
XLA Ops:
  0.6 0.8 broadcast_multiply_fusion
  1.4 0.8 copy.16
  2.4 0.8 copy.19
  3.2 0.1 reshape.121
  3.6 1.2 reduce-window.6
  4.8 0.2 slice_reduce_fusion
  5.2 2.4 scatter_custom_fusion
  7.6 5.0 gather_fusion.1
  12.7 0.7 all_to_all.25
  13.4 7.3 %all-to-all-start.1 = ((bf16[32,1,24]{2,1,0:T(2,128)(2,1)}), bf16[32,1,24]{2,1,0:T(2,128)(2,1)S(1)}, u32[]{:S(2)}, u32[]{:S(2)}) async-start(bf16[32,1,24]{2,1,0:T(2,128)(2,1)} %all_to_all.25), calls=%async_computation.1 | async-start | bytes 32768 | tf_op jit(solution)/shard_map/all_to_all | solution.py:71
  20.8 5.5 %gather_fusion.2 = bf16[768,3584]{1,0:T(8,128)(2,1)} fusion(bf16[128,3584]{1,0:T(8,128)(2,1)S(1)} %copy-done, s32[1024]{0:T(1024)S(1)} %get-tuple-element.13), kind=kCustom, calls=%fused_computation.2 | custom fusion | bytes 11013120 | tf_op jit(solution)/shard_map/gather | solution.py:60
  26.3 5.4 %gather_fusion = bf16[768,3584]{1,0:T(8,128)(2,1)} fusion(bf16[128,3584]{1,0:T(8,128)(2,1)S(1)} %copy-done.2, s32[1024]{0:T(1024)S(1)} %get-tuple-element.13), kind=kCustom, calls=%fused_computation | custom fusion | bytes 11013120 | tf_op jit(solution)/shard_map/gather | solution.py:63
  31.6 9.4 %broadcast_select_fusion.1 = (bf16[32,24,3584]{2,1,0:T(8,128)(2,1)}, bf16[32,24,3584]{2,1,0:T(8,128)(2,1)}) fusion(bf16[32,24,3584]{2,1,0:T(8,128)(2,1)} %bitcast.45, pred[32,24]{1,0:T(8,128)(4,1)S(1)} %broadcast_in_dim.36, bf16[32,24,3584]{2,1,0:T(8,128)(2,1)} %bitcast.44), kind=kLoop, calls=%fused_computation.20 | loop fusion | flops 5505024 | bytes 22020864 | tf_op jit(solution)/shard_map/jit(_where)/select_n | solution.py:63
  41.0 129.0 %all_to_all.31 = bf16[32,24,3584]{2,1,0:T(8,128)(2,1)} all-to-all(bf16[32,24,3584]{2,1,0:T(8,128)(2,1)} %get-tuple-element.9), channel_id=1, replica_groups=mesh['group'=4,'local'=8] {'group','local'}, dimensions={0} | all-to-all | bytes 11010048 | tf_op jit(solution)/shard_map/all_to_all | solution.py:69
  170.0 3.7 all-to-all-start
  174.0 11.0 %fusion.2 = f32[768,1024]{1,0:T(8,128)} fusion(bf16[768,3584]{1,0:T(8,128)(2,1)} %bitcast.47, bf16[1,3584,1024]{2,1,0:T(8,128)(2,1)} %param.11), kind=kOutput, calls=%fused_computation.10 | convolution fusion | flops 5637144576 | bytes 15990784 | tf_op jit(solution)/shard_map/dot_general | solution.py:8
  185.0 9.2 %fusion.6 = f32[768,1024]{1,0:T(8,128)} fusion(bf16[768,3584]{1,0:T(8,128)(2,1)S(1)} %bitcast.50, bf16[1,3584,1024]{2,1,0:T(8,128)(2,1)} %param.12), kind=kOutput, calls=%fused_computation.14 | convolution fusion | flops 5637144576 | bytes 15990784 | tf_op jit(solution)/shard_map/dot_general | solution.py:9
  194.2 102.7 %all-to-all-done = bf16[32,24,3584]{2,1,0:T(8,128)(2,1)} async-done(((bf16[32,24,3584]{2,1,0:T(8,128)(2,1)}), bf16[32,24,3584]{2,1,0:T(8,128)(2,1)}, u32[]{:S(2)}, u32[]{:S(2)}) %all-to-all-start) | async-done | bytes 5505056 | tf_op jit(solution)/shard_map/all_to_all | solution.py:70
  296.9 11.1 %fusion.9 = f32[768,1024]{1,0:T(8,128)} fusion(bf16[768,3584]{1,0:T(8,128)(2,1)} %bitcast.4, bf16[1,1024,3584]{2,1,0:T(8,128)(2,1)} %param.13), kind=kOutput, calls=%fused_computation.17 | convolution fusion | flops 5637144576 | bytes 15990784 | tf_op jit(solution)/shard_map/dot_general | solution.py:15
  308.0 10.3 %multiply_reduce_fusion = bf16[768]{0:T(1024)(128)(2,1)S(1)} fusion(bf16[768,3584]{1,0:T(8,128)(2,1)} %bitcast.4, bf16[1,1024,3584]{2,1,0:T(8,128)(2,1)} %param.13, f32[768,1024]{1,0:T(8,128)S(1)} %copy-done.6, f32[768,1024]{1,0:T(8,128)S(1)} %copy-done.3), kind=kOutput, calls=%fused_computation.6 | convolution fusion | flops 5650119680 | bytes 19138048 | tf_op jit(solution)/shard_map/dot_general | solution.py:13
  318.3 0.7 convert_element_type.57
  319.0 2.7 all-to-all-start.4
  321.8 16.3 %fusion = f32[768,3584]{1,0:T(8,128)} fusion(bf16[1,3584,1024]{2,1,0:T(8,128)(2,1)} %param.11, f32[768,1024]{1,0:T(8,128)} %fusion.2, f32[768,1024]{1,0:T(8,128)} %fusion.6, f32[768,1024]{1,0:T(8,128)} %fusion.9, f32[768]{0:T(1024)S(1)} %reshape.128), kind=kOutput, calls=%fused_computation.8 | convolution fusion | flops 5645795328 | bytes 27790336 | tf_op jit(solution)/shard_map/dot_general | solution.py:23
  338.1 13.2 %add_convert_fusion = bf16[768,3584]{1,0:T(8,128)(2,1)} fusion(f32[768,3584]{1,0:T(8,128)} %fusion, bf16[1,3584,1024]{2,1,0:T(8,128)(2,1)} %param.12, f32[768,1024]{1,0:T(8,128)S(1)} %copy-done.5, f32[768]{0:T(1024)S(1)} %reshape.128, f32[768,1024]{1,0:T(8,128)S(1)} %copy-done.4), kind=kOutput, calls=%fused_computation.7 | convolution fusion | flops 5648154624 | bytes 30149632 | tf_op jit(solution)/shard_map/dot_general | solution.py:26
  351.3 6.2 %all-to-all-start.3 = ((bf16[32,24,3584]{2,1,0:T(8,128)(2,1)}), bf16[32,24,3584]{2,1,0:T(8,128)(2,1)}, u32[]{:S(2)}, u32[]{:S(2)}) async-start(bf16[32,24,3584]{2,1,0:T(8,128)(2,1)} %bitcast.46), calls=%async_computation.3 | async-start | bytes 11010048 | tf_op jit(solution)/shard_map/all_to_all | solution.py:82
  357.6 3.5 gather_fusion.4
  361.1 0.1 reshape.127
  361.3 0.7 copy.22
  361.9 118.4 %all-to-all-done.3 = bf16[32,24,3584]{2,1,0:T(8,128)(2,1)} async-done(((bf16[32,24,3584]{2,1,0:T(8,128)(2,1)}), bf16[32,24,3584]{2,1,0:T(8,128)(2,1)}, u32[]{:S(2)}, u32[]{:S(2)}) %all-to-all-start.3) | async-done | bytes 5505056 | tf_op jit(solution)/shard_map/all_to_all | solution.py:82
  480.3 11.2 %gather_fusion.3 = bf16[512,3584]{1,0:T(8,128)(2,1)} fusion(bf16[768,3584]{1,0:T(8,128)(2,1)} %bitcast.11, s32[1024]{0:T(1024)S(1)} %pad_clamp_fusion), kind=kCustom, calls=%fused_computation.3 | custom fusion | bytes 7342080 | tf_op jit(solution)/shard_map/gather | solution.py:87
  491.6 7.1 %reshape.125 = bf16[128,4,3584]{2,1,0:T(4,128)(2,1)} reshape(bf16[512,3584]{1,0:T(8,128)(2,1)} %gather_fusion.3) | data formatting | bytes 7340032 | tf_op jit(solution)/shard_map/reshape | solution.py:87
  498.7 7.4 %reduce_sum.34 = bf16[128,3584]{1,0:T(8,128)(2,1)} reduce(bf16[128,4,3584]{2,1,0:T(4,128)(2,1)} %reshape.125, bf16[]{:T(256)} %constant.39.clone.1), dimensions={1}, to_apply=%region_4.5 | reduce | flops 1376256 | bytes 4587522 | tf_op jit(solution)/shard_map/reduce_sum | solution.py:88
  (40 shorter events, 1.1 us)
Async XLA Ops:
  0.6 20.1 %copy-start = (bf16[128,3584]{1,0:T(8,128)(2,1)S(1)}, bf16[128,3584]{1,0:T(8,128)(2,1)}, u32[]{:S(2)}) copy-start(bf16[128,3584]{1,0:T(8,128)(2,1)} %param.7) | copy-start | bytes 2752516
  13.4 27.6 %all-to-all-start.1 = ((bf16[32,1,24]{2,1,0:T(2,128)(2,1)}), bf16[32,1,24]{2,1,0:T(2,128)(2,1)S(1)}, u32[]{:S(2)}, u32[]{:S(2)}) async-start(bf16[32,1,24]{2,1,0:T(2,128)(2,1)} %all_to_all.25), calls=%async_computation.1 | async-start | bytes 32768 | tf_op jit(solution)/shard_map/all_to_all | solution.py:71
  20.8 5.5 %copy-start.2 = (bf16[128,3584]{1,0:T(8,128)(2,1)S(1)}, bf16[128,3584]{1,0:T(8,128)(2,1)}, u32[]{:S(2)}) copy-start(bf16[128,3584]{1,0:T(8,128)(2,1)} %param.8) | copy-start | bytes 2752516
  170.0 14.9 %slice-start = ((s8[5505024]{0:T(1024)(128)(4,1)}), s8[1310720]{0:T(1024)(128)(4,1)S(1)}, s32[]{:S(2)}) async-start(s8[5505024]{0:T(1024)(128)(4,1)} %bitcast.48), calls=%async_computation.5 | async-start | bytes 2621440
  170.0 126.9 %all-to-all-start = ((bf16[32,24,3584]{2,1,0:T(8,128)(2,1)}), bf16[32,24,3584]{2,1,0:T(8,128)(2,1)}, u32[]{:S(2)}, u32[]{:S(2)}) async-start(bf16[32,24,3584]{2,1,0:T(8,128)(2,1)} %get-tuple-element.8), calls=%async_computation | async-start | bytes 11010048 | tf_op jit(solution)/shard_map/all_to_all | solution.py:70
  173.9 11.0 %slice-start.1 = ((s8[5505024]{0:T(1024)(128)(4,1)}), s8[4194304]{0:T(1024)(128)(4,1)S(1)}, s32[]{:S(2)}) async-start(s8[5505024]{0:T(1024)(128)(4,1)} %bitcast.48), calls=%async_computation.6 | async-start | bytes 8388608
  296.9 11.1 %copy-start.3 = (f32[768,1024]{1,0:T(8,128)S(1)}, f32[768,1024]{1,0:T(8,128)}, u32[]{:S(2)}) copy-start(f32[768,1024]{1,0:T(8,128)} %fusion.2) | copy-start | bytes 9437188
  296.9 11.1 %copy-start.6 = (f32[768,1024]{1,0:T(8,128)S(1)}, f32[768,1024]{1,0:T(8,128)}, u32[]{:S(2)}) copy-start(f32[768,1024]{1,0:T(8,128)} %fusion.6) | copy-start | bytes 9437188
  319.0 32.2 %all-to-all-start.4 = ((bf16[32,1,24]{2,1,0:T(2,128)(2,1)}), bf16[32,1,24]{2,1,0:T(2,128)(2,1)S(1)}, u32[]{:S(2)}, u32[]{:S(2)}) async-start(bf16[32,1,24]{2,1,0:T(2,128)(2,1)} %convert_element_type.57), calls=%async_computation.4 | async-start | bytes 32768 | tf_op jit(solution)/shard_map/all_to_all | solution.py:83
  321.8 16.3 %copy-start.4 = (f32[768,1024]{1,0:T(8,128)S(1)}, f32[768,1024]{1,0:T(8,128)}, u32[]{:S(2)}) copy-start(f32[768,1024]{1,0:T(8,128)} %fusion.2) | copy-start | bytes 9437188
  321.8 16.3 %copy-start.5 = (f32[768,1024]{1,0:T(8,128)S(1)}, f32[768,1024]{1,0:T(8,128)}, u32[]{:S(2)}) copy-start(f32[768,1024]{1,0:T(8,128)} %fusion.9) | copy-start | bytes 9437188
  351.3 129.1 %all-to-all-start.3 = ((bf16[32,24,3584]{2,1,0:T(8,128)(2,1)}), bf16[32,24,3584]{2,1,0:T(8,128)(2,1)}, u32[]{:S(2)}, u32[]{:S(2)}) async-start(bf16[32,24,3584]{2,1,0:T(8,128)(2,1)} %bitcast.46), calls=%async_computation.3 | async-start | bytes 11010048 | tf_op jit(solution)/shard_map/all_to_all | solution.py:82
  491.6 14.5 %copy-start.1 = (bf16[128,3584]{1,0:T(8,128)(2,1)S(1)}, bf16[128,3584]{1,0:T(8,128)(2,1)}, u32[]{:S(2)}) copy-start(bf16[128,3584]{1,0:T(8,128)(2,1)} %param.7) | copy-start | bytes 2752516
where the time goes:
time: 507 us; the launch traced here: 506 us
  waiting for transfers between devices  221 us (44%)
  blocking collectives  129 us (25%)
  matrix products  71.1 us (14%)
  local copies, waits for them, and re-layouts  45 us (9%)
  starting transfers between devices  19.9 us (4%)
  other arithmetic  19 us (4%)
    all_to_all x1, blocking collectives, local(): lax.all_to_all(send_x, ('group', 'local'), split_axis=0, concat_axis=0, t...  129 us
    all_to_all x1, waiting for transfers between devices, local(): lax.all_to_all(contrib, ('group', 'local'), split_axis=0, concat_axis=0,...  118 us
    all_to_all x1, waiting for transfers between devices, local(): lax.all_to_all(send_dy, ('group', 'local'), split_axis=0, concat_axis=0,...  103 us
    dot_general x1, matrix products, expert_rows(): lax.dot_general(grad_gate, gate_mat, (((1,), (1,)), ((), ())), preferred_...  16.3 us
    dot_general x1, matrix products, expert_rows(): lax.dot_general(grad_up, up_mat, (((1,), (1,)), ((), ())), preferred_elem...  13.2 us
    gather x1, local copies, waits for them, and re-layouts, local(): terms = back_rows[slot_of].reshape(token_rows, top_count, model_width)  11.2 us
    dot_general x1, matrix products, expert_rows(): lax.dot_general(rows_dy, down_mat, (((1,), (1,)), ((), ())), preferred_el...  11.1 us
    dot_general x1, matrix products, expert_rows(): gate_pre = jnp.dot(rows_x, gate_mat, preferred_element_type=jnp.float32)  11 us
  transfers between devices with their start and end apart: 4, of which 2 were waited for; matrix products, arithmetic and copies ran while one was open for 15% of the time, Pallas kernels for 0%

commit v1 on v0

v1 whole, which is shorter than its diff:
```python
import jax
import jax.numpy as jnp
from jax import lax
from jax.sharding import PartitionSpec as P

F32 = jnp.float32
BF16 = jnp.bfloat16


def dot_t(left, right):
    return lax.dot_general(left, right, (((1,), (1,)), ((), ())), preferred_element_type=F32)


def forward_rows(rows_x, gate_mat, up_mat):
    gate_pre = jnp.dot(rows_x, gate_mat, preferred_element_type=F32)
    up_pre = jnp.dot(rows_x, up_mat, preferred_element_type=F32)
    return gate_pre, up_pre


def backward_rows(gate_pre, up_pre, rows_dy, gate_mat, up_mat, down_mat):
    back = dot_t(rows_dy, down_mat)
    sigmoid_gate = jax.nn.sigmoid(gate_pre)
    active = gate_pre * sigmoid_gate
    hidden = (active * up_pre).astype(BF16)
    grad_weight = jnp.sum(hidden.astype(F32) * back, axis=1).astype(BF16)
    grad_gate = (back * up_pre * sigmoid_gate * (1.0 + gate_pre * (1.0 - sigmoid_gate))).astype(BF16)
    grad_up = (back * active).astype(BF16)
    contrib = (dot_t(grad_gate, gate_mat) + dot_t(grad_up, up_mat)).astype(BF16)
    return contrib, grad_weight


def local(tokens, grad_out, expert_ids, combine, gate_weight, up_weight, down_weight):
    token_rows, model_width = tokens.shape
    top_count = expert_ids.shape[1]
    group_count = lax.axis_size("group")
    local_count = lax.axis_size("local")
    expert_count = group_count * local_count
    mean_pair = token_rows * top_count // expert_count
    pair_cap = mean_pair + (mean_pair + 1) // 2
    my_group = lax.axis_index("group")
    my_local = lax.axis_index("local")
    gate_mat, up_mat, down_mat = gate_weight[0], up_weight[0], down_weight[0]
    column_rows = local_count * token_rows
    pair_rows = local_count * pair_cap

    all_ids = lax.all_gather(expert_ids, "local", axis=0, tiled=True)
    all_combine = lax.all_gather(combine, "local", axis=0, tiled=True)
    all_x = lax.all_gather(tokens, "local", axis=0, tiled=True)
    all_dy = lax.all_gather(grad_out, "local", axis=0, tiled=True)

    partners = my_group ^ jnp.arange(group_count, dtype=jnp.int32)
    wanted = partners * local_count + my_local
    hit = all_ids[None, :, :] == wanted[:, None, None]
    named = jnp.any(hit, axis=2)
    weight = jnp.sum(jnp.where(hit, all_combine[None].astype(F32), 0.0), axis=2)
    counts = named.astype(jnp.int32).reshape(group_count, local_count, token_rows)
    rank = jnp.cumsum(counts, axis=2) - 1
    base = jnp.arange(local_count, dtype=jnp.int32)[None, :, None] * pair_cap
    slot = jnp.where(counts > 0, rank + base, -1).reshape(group_count, column_rows)
    slots = jnp.arange(pair_rows, dtype=jnp.int32)
    pick = slot[:, None, :] == slots[None, :, None]
    select = pick.astype(BF16)
    scatter = jnp.where(pick, weight[:, None, :], 0.0).astype(BF16)

    def swap(value, j):
        if j == 0:
            return value
        return lax.ppermute(value, "group", [(i, i ^ j) for i in range(group_count)])

    order = [j for j in range(group_count - 1, 0, -1)] + [0]

    def spread(column):
        moved = {}
        for j in order:
            rows = jnp.dot(select[j], column, preferred_element_type=F32).astype(BF16)
            moved[j] = swap(rows, j)
        return moved

    rows_x = spread(all_x)
    rows_dy = spread(all_dy)
    consume = [0] + [j for j in range(1, group_count)]
    pre = {j: forward_rows(rows_x[j], gate_mat, up_mat) for j in consume}
    back_rows, weights = {}, {}
    for j in consume:
        contrib, weights[j] = backward_rows(*pre[j], rows_dy[j], gate_mat, up_mat, down_mat)
        back_rows[j] = swap(contrib, j)

    total = lax.dot_general(
        scatter.reshape(group_count * pair_rows, column_rows),
        jnp.concatenate([back_rows[j] for j in range(group_count)], axis=0),
        (((0,), (0,)), ((), ())),
        preferred_element_type=F32,
    ).astype(BF16)
    grad_tokens = lax.psum_scatter(total, "local", scatter_dimension=0, tiled=True)

    grad_weight = jnp.stack([weights[j] for j in range(group_count)])[partners]
    grad_weight = grad_weight.reshape(expert_count, pair_cap)
    back_weight = lax.all_to_all(
        grad_weight, ("group", "local"), split_axis=0, concat_axis=0, tiled=True
    )
    flat_ids = expert_ids.reshape(-1)
    one_hot = flat_ids[:, None] == jnp.arange(expert_count, dtype=jnp.int32)[None, :]
    ranks = jnp.cumsum(one_hot.astype(jnp.int32), axis=0) - 1
    chosen = one_hot[:, :, None] & (
        ranks[:, :, None] == jnp.arange(pair_cap, dtype=jnp.int32)[None, None, :]
    )
    grad_combine = jnp.sum(jnp.where(chosen, back_weight[None].astype(F32), 0.0), axis=(1, 2))
    return grad_tokens, grad_combine.astype(BF16).reshape(token_rows, top_count)


def solution(mesh):
    rows = P(("group", "local"), None)
    mats = P(("group", "local"), None, None)
    return jax.shard_map(
        local,
        mesh=mesh,
        in_specs=(rows, rows, rows, rows, mats, mats, mats),
        out_specs=(rows, rows),
        check_vma=False,
    )
```

time: 507 us -> 521 us (1.028); the launches traced: 506 us -> 511 us
  waiting for transfers between devices: 221 us -> 331 us
  blocking collectives: 129 us -> 26.7 us
  matrix products: 71.1 us -> 116 us
  local copies, waits for them, and re-layouts: 45 us -> 3.47 us
  other arithmetic: 19 us -> 4.02 us
  between operations: 0.84 us -> 14.5 us
    all_to_all x3 -> x0, waiting for transfers between devices: 221 us -> none  [the longest x1 118 us: local(): lax.all_to_all(contrib, ('group', 'local'), split_axis=0, concat_axis=0,...]
    ppermute x0 -> x9, waiting for transfers between devices: none -> 150 us  [swap(): lax.ppermute(value, 'group', [(i, i ^ j) for i in range(group_count)])]
    all_to_all x1 -> x0, blocking collectives: 129 us -> none  [local(): lax.all_to_all(send_x, ('group', 'local'), split_axis=0, concat_axis=0, t...]
    all_gather x0 -> x2, waiting for transfers between devices: none -> 109 us  [the longest x1 60.9 us: local(): all_dy = lax.all_gather(grad_out, 'local', axis=0, tiled=True)]
    reduce_scatter x0 -> x1, waiting for transfers between devices: none -> 63.1 us  [local(): lax.psum_scatter(total, 'local', scatter_dimension=0, tiled=True)]
    dot_general x6 -> x28, matrix products: 71.1 us -> 116 us  [the longest x12 51.4 us: dot_t(): lax.dot_general(left, right, (((1,), (1,)), ((), ())), preferred_element_...]
    gather x5 -> x1, local copies, waits for them, and re-layouts: 30.6 us -> 0.57 us  [local(): grad_weight = jnp.stack([weights[j] for j in range(group_count)])[partners]]
    all_gather x0 -> x2, blocking collectives: none -> 26.7 us  [the longest x1 13.7 us: local(): all_combine = lax.all_gather(combine, 'local', axis=0, tiled=True)]
  transfers between devices with their start and end apart: 4 -> 13, of which waited for: 2 -> 8; matrix products, arithmetic and copies ran while one was open for 15% -> 21% of each run, Pallas kernels for 0% -> 0%
where the time goes in v1:
time: 521 us; the launch traced here: 511 us
  waiting for transfers between devices  331 us (64%)
  matrix products  116 us (22%)
  blocking collectives  26.7 us (5%)
  starting transfers between devices  14.9 us (3%)
  between operations  14.5 us (3%)
    ppermute x9, waiting for transfers between devices, swap(): lax.ppermute(value, 'group', [(i, i ^ j) for i in range(group_count)])  150 us
    reduce_scatter x1, waiting for transfers between devices, local(): lax.psum_scatter(total, 'local', scatter_dimension=0, tiled=True)  63.1 us
    all_gather x1, waiting for transfers between devices, local(): all_dy = lax.all_gather(grad_out, 'local', axis=0, tiled=True)  60.9 us
    dot_general x12, matrix products, dot_t(): lax.dot_general(left, right, (((1,), (1,)), ((), ())), preferred_element_...  51.4 us
    all_gather x1, waiting for transfers between devices, local(): all_x = lax.all_gather(tokens, 'local', axis=0, tiled=True)  48.1 us
    dot_general x7, matrix products, spread(): rows = jnp.dot(select[j], column, preferred_element_type=F32).astype(BF16)  27.6 us
    dot_general x4, matrix products, forward_rows(): gate_pre = jnp.dot(rows_x, gate_mat, preferred_element_type=F32)  16.4 us
    all_gather x1, blocking collectives, local(): all_combine = lax.all_gather(combine, 'local', axis=0, tiled=True)  13.7 us
  transfers between devices with their start and end apart: 13, of which 8 were waited for; matrix products, arithmetic and copies ran while one was open for 21% of the time, Pallas kernels for 0%

profile of v1, /device:TPU:0, one launch (start us, length us, event | category | flops | bytes accessed | tf_op | source)
XLA Modules:
  0.0 511.1 jit_solution(8746710838023505817)
XLA Ops:
  8.8 13.7 %all_gather.13 = bf16[1024,4]{0,1:T(4,128)(2,1)S(1)} all-gather(bf16[128,4]{0,1:T(4,128)(2,1)} %param.10), channel_id=1, replica_groups=mesh['group'=4,'local'=8] {'local'}, dimensions={0}, use_global_device_ids=true | all-gather | bytes 9216 | tf_op jit(solution)/shard_map/all_gather | solution.py:47
  22.5 13.0 %all_gather.12 = s32[1024,4]{0,1:T(4,128)S(1)} all-gather(s32[128,4]{0,1:T(4,128)} %param.9), channel_id=1, replica_groups=mesh['group'=4,'local'=8] {'local'}, dimensions={0}, use_global_device_ids=true | all-gather | bytes 18432 | tf_op jit(solution)/shard_map/all_gather | solution.py:46
  37.8 48.1 %all-gather.5.cloned.1.call-done = bf16[1024,3584]{1,0:T(8,128)(2,1)} async-done(((bf16[128,3584]{1,0:T(8,128)(2,1)}), bf16[1024,3584]{1,0:T(8,128)(2,1)}) %all-gather.5.cloned.1.call-update) | async-done | bytes 7340048 | tf_op jit(solution)/shard_map/all_gather | solution.py:48
  85.9 4.9 convolution_convert_fusion.7
  90.8 5.3 %fusion.14 = f32[192,1024]{1,0:T(8,128)S(1)} fusion(bf16[192,3584]{1,0:T(8,128)(2,1)S(1)} %convolution_convert_fusion.7, bf16[1,3584,1024]{2,1,0:T(8,128)(2,1)} %param.11), kind=kOutput, calls=%fused_computation.16 | convolution fusion | flops 1409286144 | bytes 9502720 | tf_op jit(solution)/shard_map/dot_general | solution.py:15
  98.6 60.9 %all-gather.3.cloned.1.call-done = bf16[1024,3584]{1,0:T(8,128)(2,1)} async-done(((bf16[128,3584]{1,0:T(8,128)(2,1)}), bf16[1024,3584]{1,0:T(8,128)(2,1)}) %all-gather.3.cloned.1.call-update) | async-done | bytes 7340048 | tf_op jit(solution)/shard_map/all_gather | solution.py:49
  159.5 6.0 %convolution_convert_fusion.6 = bf16[192,3584]{1,0:T(8,128)(2,1)} fusion(bf16[1024,3584]{1,0:T(8,128)(2,1)} %all-gather.3.cloned.1.call-done, pred[4,192,1024]{2,1,0:T(32,128)(4,1)S(1)} %iota_compare_fusion), kind=kOutput, calls=%fused_computation.62 | convolution fusion | flops 1409974272 | bytes 8912896 | tf_op jit(solution)/shard_map/dot_general | solution.py:75
  167.0 2.9 convolution_convert_fusion.4
  171.4 2.8 convolution_convert_fusion.2
  174.8 2.8 convolution_convert_fusion.5
  179.1 3.2 convolution_convert_fusion.1
  183.8 9.5 %multiply_reduce_fusion.3 = (bf16[192]{0:T(256)(128)(2,1)S(1)}, f32[192,1024]{1,0:T(8,128)S(1)}) fusion(f32[192,1024]{1,0:T(8,128)} %fusion.30, f32[192,1024]{1,0:T(8,128)S(1)} %fusion.14, bf16[1,1024,3584]{2,1,0:T(8,128)(2,1)} %param.13, bf16[1024,3584]{1,0:T(8,128)(2,1)} %all-gather.3.cloned.1.call-done, pred[4,192,1024]{2,1,0:T(32,128)(4,1)} %copy-done), kind=kOutput, calls=%fused_computation.78 | convolution fusion | flops 2821029632 | bytes 17236352 | tf_op jit(solution)/shard_map/dot_general | solution.py:11
  193.3 4.9 convolution_convert_fusion.3
  198.2 89.4 %collective-permute-done.7 = bf16[192,3584]{1,0:T(8,128)(2,1)} collective-permute-done((bf16[192,3584]{1,0:T(8,128)(2,1)}, bf16[192,3584]{1,0:T(8,128)(2,1)}, u32[]{:S(2)}, u32[]{:S(2)}) %collective-permute-start.7) | collective-permute-done | bytes 1376288 | tf_op jit(solution)/shard_map/ppermute | solution.py:68
  288.2 5.2 %fusion.2 = f32[192,1024]{1,0:T(8,128)S(1)} fusion(bf16[192,3584]{1,0:T(8,128)(2,1)} %collective-permute-done.7, bf16[1,3584,1024]{2,1,0:T(8,128)(2,1)} %param.11), kind=kOutput, calls=%fused_computation.4 | convolution fusion | flops 1409286144 | bytes 9502720 | tf_op jit(solution)/shard_map/dot_general | solution.py:15
  293.4 3.1 fusion.18
  296.5 6.1 %multiply_reduce_fusion = (bf16[192]{0:T(256)(128)(2,1)S(1)}, f32[192,1024]{1,0:T(8,128)S(1)}) fusion(f32[192,1024]{1,0:T(8,128)S(1)} %fusion.18, f32[192,1024]{1,0:T(8,128)S(1)} %fusion.2, bf16[192,3584]{1,0:T(8,128)(2,1)} %collective-permute-done.6, bf16[1,1024,3584]{2,1,0:T(8,128)(2,1)} %param.13), kind=kOutput, calls=%fused_computation.72 | convolution fusion | flops 1411055360 | bytes 11075968 | tf_op jit(solution)/shard_map/dot_general | solution.py:11
  310.6 38.2 %collective-permute-done.4 = bf16[192,3584]{1,0:T(8,128)(2,1)} collective-permute-done((bf16[192,3584]{1,0:T(8,128)(2,1)S(1)}, bf16[192,3584]{1,0:T(8,128)(2,1)}, u32[]{:S(2)}, u32[]{:S(2)}) %collective-permute-start.4) | collective-permute-done | bytes 1376288 | tf_op jit(solution)/shard_map/ppermute | solution.py:68
  348.8 2.9 fusion.6
  351.7 2.9 fusion.22
  354.6 6.1 %multiply_reduce_fusion.1 = (bf16[192]{0:T(256)(128)(2,1)S(1)}, f32[192,1024]{1,0:T(8,128)S(1)}) fusion(f32[192,1024]{1,0:T(8,128)S(1)} %fusion.22, f32[192,1024]{1,0:T(8,128)S(1)} %fusion.6, bf16[192,3584]{1,0:T(8,128)(2,1)} %collective-permute-done.3, bf16[1,1024,3584]{2,1,0:T(8,128)(2,1)} %param.13), kind=kOutput, calls=%fused_computation.74 | convolution fusion | flops 1411055360 | bytes 11075968 | tf_op jit(solution)/shard_map/dot_general | solution.py:11
  366.6 2.9 fusion.10
  369.5 2.9 fusion.26
  372.4 6.4 %multiply_reduce_fusion.2 = (bf16[192]{0:T(256)(128)(2,1)S(1)}, f32[192,1024]{1,0:T(8,128)S(1)}) fusion(f32[192,1024]{1,0:T(8,128)S(1)} %fusion.26, f32[192,1024]{1,0:T(8,128)S(1)} %fusion.10, bf16[192,3584]{1,0:T(8,128)(2,1)} %collective-permute-done, bf16[1,1024,3584]{2,1,0:T(8,128)(2,1)} %param.13), kind=kOutput, calls=%fused_computation.76 | convolution fusion | flops 1411055360 | bytes 11075968 | tf_op jit(solution)/shard_map/dot_general | solution.py:11
  381.5 3.7 fusion.65
  386.7 3.8 fusion.12
  393.1 3.7 collective-permute-done.5
  396.7 19.1 %collective-permute-done.2 = bf16[192,3584]{1,0:T(8,128)(2,1)} collective-permute-done((bf16[192,3584]{1,0:T(8,128)(2,1)}, bf16[192,3584]{1,0:T(8,128)(2,1)}, u32[]{:S(2)}, u32[]{:S(2)}) %collective-permute-start.2) | collective-permute-done | bytes 1376288 | tf_op jit(solution)/shard_map/ppermute | solution.py:68
  415.8 9.7 %convolution_convert_fusion = bf16[1024,3584]{1,0:T(8,128)(2,1)} fusion(bf16[768,1024]{1,0:T(8,128)(2,1)S(1)} %fusion.71, bf16[192,3584]{1,0:T(8,128)(2,1)} %collective-permute-done.8, bf16[192,3584]{1,0:T(8,128)(2,1)} %collective-permute-done.5, bf16[192,3584]{1,0:T(8,128)(2,1)} %collective-permute-done.2, bf16[192,3584]{1,0:T(8,128)(2,1)S(1)} %fusion.68), kind=kOutput, calls=%fused_computation.1 | convolution fusion | flops 5662834688 | bytes 14417920 | tf_op jit(solution)/shard_map/dot_general | solution.py:88
  429.4 3.2 all-to-all-start
  432.6 7.2 %all-to-all-done = bf16[32,1,24]{2,1,0:T(2,128)(2,1)S(1)} async-done(((bf16[32,1,24]{2,1,0:T(2,128)(2,1)}), bf16[32,1,24]{2,1,0:T(2,128)(2,1)S(1)}, u32[]{:S(2)}, u32[]{:S(2)}) %all-to-all-start) | async-done | bytes 1568 | tf_op jit(solution)/shard_map/all_to_all | solution.py:98
  441.1 63.1 %reduce-scatter.2.cloned.1.call-done = bf16[128,3584]{1,0:T(8,128)(2,1)} async-done(((bf16[1024,3584]{1,0:T(8,128)(2,1)}), bf16[128,3584]{1,0:T(8,128)(2,1)}) %reduce-scatter.2.cloned.1.call-update) | async-done | bytes 917520 | tf_op jit(solution)/shard_map/reduce_scatter | solution.py:94
  (91 shorter events, 38.8 us)
Async XLA Ops:
  7.2 78.7 %all-gather.5.cloned.1.call-start = ((), (), s32[]{:S(2)}) async-start(), calls=%async_computation.3 | async-start | bytes 8257536 | tf_op jit(solution)/shard_map/all_gather | solution.py:48
  7.9 151.6 %all-gather.3.cloned.1.call-start = ((), (), s32[]{:S(2)}) async-start(), calls=%async_computation.2 | async-start | bytes 8257536 | tf_op jit(solution)/shard_map/all_gather | solution.py:49
  8.6 495.6 %reduce-scatter.2.cloned.1.call-start = ((), (), s32[]{:S(2)}) async-start(), calls=%async_computation.4 | async-start | bytes 8257536 | tf_op jit(solution)/shard_map/reduce_scatter | solution.py:94
  37.8 141.3 %copy-start = (pred[4,192,1024]{2,1,0:T(32,128)(4,1)}, pred[4,192,1024]{2,1,0:T(32,128)(4,1)S(1)}, u32[]{:S(2)}) copy-start(pred[4,192,1024]{2,1,0:T(32,128)(4,1)S(1)} %iota_compare_fusion) | copy-start | bytes 2359300
  85.9 10.2 %slice-start = ((s8[7340032]{0:T(1024)(128)(4,1)}), s8[3145728]{0:T(1024)(128)(4,1)S(1)}, s32[]{:S(2)}) async-start(s8[7340032]{0:T(1024)(128)(4,1)} %bitcast.137), calls=%async_computation.5 | async-start | bytes 6291456
  90.8 5.3 %slice-start.1 = ((s8[7340032]{0:T(1024)(128)(4,1)}), s8[4194304]{0:T(1024)(128)(4,1)S(1)}, s32[]{:S(2)}) async-start(s8[7340032]{0:T(1024)(128)(4,1)} %bitcast.137), calls=%async_computation.6 | async-start | bytes 8388608
  159.5 7.5 %copy-start.2 = (bf16[1024,3584]{1,0:T(8,128)(2,1)S(1)}, bf16[1024,3584]{1,0:T(8,128)(2,1)}, u32[]{:S(2)}) copy-start(bf16[1024,3584]{1,0:T(8,128)(2,1)} %all-gather.3.cloned.1.call-done) | copy-start | bytes 22020100
  165.5 206.9 %collective-permute-start = (bf16[192,3584]{1,0:T(8,128)(2,1)}, bf16[192,3584]{1,0:T(8,128)(2,1)}, u32[]{:S(2)}, u32[]{:S(2)}) collective-permute-start(bf16[192,3584]{1,0:T(8,128)(2,1)} %convolution_convert_fusion.6), channel_id=1, source_target_pairs={{0,8},{8,0},{16,24},{24,16},{1,9},{9,1},{17,25},{25,17},{2,10},{10... | collective-permute-start | bytes 4128776 | tf_op jit(solution)/shard_map/ppermute | solution.py:68
  167.0 7.7 %slice-start.6 = ((s8[7340032]{0:T(1024)(128)(4,1)}), s8[4194304]{0:T(1024)(128)(4,1)S(1)}, s32[]{:S(2)}) async-start(s8[7340032]{0:T(1024)(128)(4,1)} %bitcast.145), calls=%async_computation.11 | async-start | bytes 8388608
  169.9 4.8 slice-start.7
  169.9 184.7 %collective-permute-start.3 = (bf16[192,3584]{1,0:T(8,128)(2,1)}, bf16[192,3584]{1,0:T(8,128)(2,1)}, u32[]{:S(2)}, u32[]{:S(2)}) collective-permute-start(bf16[192,3584]{1,0:T(8,128)(2,1)} %convolution_convert_fusion.4), channel_id=1, source_target_pairs={{0,16},{8,24},{16,0},{24,8},{1,17},{9,25},{17,1},{25,9},{2,18},{10... | collective-permute-start | bytes 4128776 | tf_op jit(solution)/shard_map/ppermute | solution.py:68
  174.2 122.3 %collective-permute-start.6 = (bf16[192,3584]{1,0:T(8,128)(2,1)}, bf16[192,3584]{1,0:T(8,128)(2,1)}, u32[]{:S(2)}, u32[]{:S(2)}) collective-permute-start(bf16[192,3584]{1,0:T(8,128)(2,1)} %convolution_convert_fusion.2), channel_id=1, source_target_pairs={{0,24},{8,16},{16,8},{24,0},{1,25},{9,17},{17,9},{25,1},{2,26},{10... | collective-permute-start | bytes 4128776 | tf_op jit(solution)/shard_map/ppermute | solution.py:68
  177.6 189.0 %collective-permute-start.1 = (bf16[192,3584]{1,0:T(8,128)(2,1)}, bf16[192,3584]{1,0:T(8,128)(2,1)}, u32[]{:S(2)}, u32[]{:S(2)}) collective-permute-start(bf16[192,3584]{1,0:T(8,128)(2,1)} %convolution_convert_fusion.5), channel_id=1, source_target_pairs={{0,8},{8,0},{16,24},{24,16},{1,9},{9,1},{17,25},{25,17},{2,10},{10... | collective-permute-start | bytes 4128776 | tf_op jit(solution)/shard_map/ppermute | solution.py:68
  182.3 105.3 %collective-permute-start.7 = (bf16[192,3584]{1,0:T(8,128)(2,1)}, bf16[192,3584]{1,0:T(8,128)(2,1)}, u32[]{:S(2)}, u32[]{:S(2)}) collective-permute-start(bf16[192,3584]{1,0:T(8,128)(2,1)} %convolution_convert_fusion.1), channel_id=1, source_target_pairs={{0,24},{8,16},{16,8},{24,0},{1,25},{9,17},{17,9},{25,1},{2,26},{10... | collective-permute-start | bytes 4128776 | tf_op jit(solution)/shard_map/ppermute | solution.py:68
  193.3 100.1 %slice-start.2 = ((s8[7340032]{0:T(1024)(128)(4,1)}), s8[4194304]{0:T(1024)(128)(4,1)S(1)}, s32[]{:S(2)}) async-start(s8[7340032]{0:T(1024)(128)(4,1)} %bitcast.139), calls=%async_computation.7 | async-start | bytes 8388608
  198.2 95.2 %slice-start.3 = ((s8[7340032]{0:T(1024)(128)(4,1)}), s8[3145728]{0:T(1024)(128)(4,1)S(1)}, s32[]{:S(2)}) async-start(s8[7340032]{0:T(1024)(128)(4,1)} %bitcast.139), calls=%async_computation.8 | async-start | bytes 6291456
  287.6 61.1 %collective-permute-start.4 = (bf16[192,3584]{1,0:T(8,128)(2,1)S(1)}, bf16[192,3584]{1,0:T(8,128)(2,1)}, u32[]{:S(2)}, u32[]{:S(2)}) collective-permute-start(bf16[192,3584]{1,0:T(8,128)(2,1)S(1)} %convolution_convert_fusion.3), channel_id=1, source_target_pairs={{0,16},{8,24},{16,0},{24,8},{1,17},{9,25},{17,1},{25,9},{2,18},{10... | collective-permute-start | bytes 4128776 | tf_op jit(solution)/shard_map/ppermute | solution.py:68
  288.2 14.5 %slice-start.4 = ((s8[7340032]{0:T(1024)(128)(4,1)}), s8[4194304]{0:T(1024)(128)(4,1)S(1)}, s32[]{:S(2)}) async-start(s8[7340032]{0:T(1024)(128)(4,1)} %bitcast.141), calls=%async_computation.9 | async-start | bytes 8388608
  293.4 9.3 %slice-start.5 = ((s8[7340032]{0:T(1024)(128)(4,1)}), s8[3145728]{0:T(1024)(128)(4,1)S(1)}, s32[]{:S(2)}) async-start(s8[7340032]{0:T(1024)(128)(4,1)} %bitcast.141), calls=%async_computation.10 | async-start | bytes 6291456
  308.1 85.0 %collective-permute-start.8 = (bf16[192,3584]{1,0:T(8,128)(2,1)S(1)}, bf16[192,3584]{1,0:T(8,128)(2,1)}, u32[]{:S(2)}, u32[]{:S(2)}) collective-permute-start(bf16[192,3584]{1,0:T(8,128)(2,1)S(1)} %fusion.59), channel_id=1, source_target_pairs={{0,24},{8,16},{16,8},{24,0},{1,25},{9,17},{17,9},{25,1},{2,26},{10... | collective-permute-start | bytes 4128776 | tf_op jit(solution)/shard_map/ppermute | solution.py:68
  366.0 30.8 %collective-permute-start.5 = (bf16[192,3584]{1,0:T(8,128)(2,1)S(1)}, bf16[192,3584]{1,0:T(8,128)(2,1)}, u32[]{:S(2)}, u32[]{:S(2)}) collective-permute-start(bf16[192,3584]{1,0:T(8,128)(2,1)S(1)} %fusion.62), channel_id=1, source_target_pairs={{0,16},{8,24},{16,0},{24,8},{1,17},{9,25},{17,1},{25,9},{2,18},{10... | collective-permute-start | bytes 4128776 | tf_op jit(solution)/shard_map/ppermute | solution.py:68
  385.2 30.6 %collective-permute-start.2 = (bf16[192,3584]{1,0:T(8,128)(2,1)}, bf16[192,3584]{1,0:T(8,128)(2,1)}, u32[]{:S(2)}, u32[]{:S(2)}) collective-permute-start(bf16[192,3584]{1,0:T(8,128)(2,1)} %fusion.65), channel_id=1, source_target_pairs={{0,8},{8,0},{16,24},{24,16},{1,9},{9,1},{17,25},{25,17},{2,10},{10... | collective-permute-start | bytes 4128776 | tf_op jit(solution)/shard_map/ppermute | solution.py:68
  425.5 0.7 copy-start.1
  429.4 10.4 %all-to-all-start = ((bf16[32,1,24]{2,1,0:T(2,128)(2,1)}), bf16[32,1,24]{2,1,0:T(2,128)(2,1)S(1)}, u32[]{:S(2)}, u32[]{:S(2)}) async-start(bf16[32,1,24]{2,1,0:T(2,128)(2,1)} %all_to_all.8), calls=%async_computation.1 | async-start | bytes 32768 | tf_op jit(solution)/shard_map/all_to_all | solution.py:98
Sparse Core Ops, SparseCore 0:
  9.6 76.1 all-gather.4
  87.5 71.9 all-gather.2
  425.6 78.5 reduce-scatter.1
